TPU v7x, 32 devices: a whole 2x2x4 slice. The times are simulated.
32 devices in a mesh: outer: 4 (over z), inner: 4 (over x, core), head: 2 (over y).
Axes of the slice: x: 2, y: 2, z: 4, core: 2. Of those that a mesh axis runs over, the one named last changes fastest.
Arguments:
- queries: bfloat16 [4096, 4096], P(('outer', 'inner', 'head')), may hold values from -6 to 6
- keys: bfloat16 [4096, 512], P(('outer', 'inner', 'head')), may hold values from -6 to 6
- values: bfloat16 [4096, 512], P(('outer', 'inner', 'head')), may hold values from -6 to 6
- doc_lengths: int32 [256], replicated, may hold values from 1 to 256, 4096 in all
Outputs:
- attended: bfloat16 [4096, 4096], P(('outer', 'inner', 'head'))
Inputs may be any that keep to these rules, and one draw needn't show every extreme that they name: `doc_lengths`: the documents lie end to end in order of position; the lengths sum to 4096 and the largest is exactly 256.
All inputs are finite; a program needn't handle non-finite values.
Results may differ from a plain program's by a relative error of at most 0.0019.
Values may be sent and summed in bfloat16 or wider, within the bound.
A program may use at most 64 MiB of HBM per device.

v0:
```python
import functools
import math

import jax
import jax.numpy as jnp
from jax import lax
from jax.experimental import pallas as pl
from jax.experimental.pallas import tpu as pltpu
from jax.sharding import PartitionSpec as P

HEAD_WIDTH = 128
DOCUMENT_SPAN = 2
QUERY_PER_KEY = 8
LANES = 128

NEG = -1e30


def piece_to_device(piece, contexts, inner_count, per_block):
    block, sub = piece // per_block, piece % per_block
    front = block < contexts
    context = jnp.where(front, block, 2 * contexts - 1 - block)
    head = jnp.where(front, sub, per_block + sub)
    return (context // inner_count, context % inner_count, head)


def document_starts(lengths, positions):
    lane = lax.broadcasted_iota(jnp.int32, lengths.shape, 1)
    within = lengths
    step = 1
    while step < LANES:
        within = within + jnp.where(lane >= step, pltpu.roll(within, step, 1), 0)
        step *= 2
    before = jnp.zeros((1, 1), jnp.int32)
    starts = jnp.zeros(positions.shape, jnp.int32)
    for row in range(lengths.shape[0]):
        ends = before + within[row : row + 1, :]
        starts = jnp.maximum(starts, jnp.where(ends <= positions, ends, 0))
        before = ends[:, LANES - 1 :]
    return jnp.max(starts, axis=1, keepdims=True)


def kernel(sizes, q_hbm, k_hbm, v_hbm, len_ref, o_hbm, q_buf, k_buf, v_buf, o_buf, bias,
           send_sem, recv_sem, in_sem, out_sem):
    outer_count, inner_count, head_count = sizes
    rows, kv_width = k_hbm.shape
    key_heads = kv_width // HEAD_WIDTH
    contexts = outer_count * inner_count
    per_block = head_count // 2
    reach = DOCUMENT_SPAN * rows * per_block
    hops = reach // rows
    pieces = contexts * head_count
    own_rows = k_buf.shape[0] - reach

    context = lax.axis_index("outer") * inner_count + lax.axis_index("inner")
    head = lax.axis_index("head")
    half, sub = head // per_block, head % per_block
    block = jnp.where(half == 0, context, 2 * contexts - 1 - context)
    piece = block * per_block + sub
    place = functools.partial(
        piece_to_device, contexts=contexts, inner_count=inner_count, per_block=per_block)
    following = place(lax.rem(piece + 1, pieces))
    preceding = place(lax.rem(piece + pieces - 1, pieces))

    barrier = pltpu.get_barrier_semaphore()
    pl.semaphore_signal(barrier, inc=1, device_id=preceding, device_id_type=pl.DeviceIdType.MESH)

    local_copies = [
        pltpu.make_async_copy(k_hbm, k_buf.at[pl.ds(reach, rows), :], in_sem.at[0]),
        pltpu.make_async_copy(v_hbm, v_buf.at[pl.ds(reach, rows), :], in_sem.at[1]),
        pltpu.make_async_copy(q_hbm, q_buf, in_sem.at[2]),
    ]
    for copy in local_copies:
        copy.start()

    def passing(hop, group):
        columns = pl.ds(group * HEAD_WIDTH, HEAD_WIDTH)
        found = []
        for at, (hbm, buf) in enumerate(((k_hbm, k_buf), (v_hbm, v_buf))):
            if hop == 0:
                source = hbm.at[:, columns]
            else:
                source = buf.at[pl.ds(reach - hop * rows, rows), columns]
            found.append(pltpu.make_async_remote_copy(
                src_ref=source,
                dst_ref=buf.at[pl.ds(reach - (hop + 1) * rows, rows), columns],
                send_sem=send_sem.at[hop, group, at],
                recv_sem=recv_sem.at[hop, group, at],
                device_id=following,
                device_id_type=pl.DeviceIdType.MESH,
            ))
        return found

    copies = [[passing(hop, group) for group in range(key_heads)] for hop in range(hops)]
    pl.semaphore_wait(barrier, 1)
    for group in range(key_heads):
        for copy in copies[0][group]:
            copy.start()

    position = piece * rows + lax.broadcasted_iota(jnp.int32, (rows, LANES), 0)
    starts = document_starts(len_ref[...], position)
    row_at = lax.broadcasted_iota(jnp.int32, (rows, reach), 0)
    column_at = lax.broadcasted_iota(jnp.int32, (rows, reach), 1)
    key_position = piece * rows + column_at - jnp.where(column_at <= row_at, 0, reach)
    bias[...] = jnp.where(key_position >= starts, 0.0, NEG)
    if own_rows > rows:
        k_buf[reach + rows :, :] = jnp.zeros((own_rows - rows, kv_width), k_buf.dtype)
        v_buf[reach + rows :, :] = jnp.zeros((own_rows - rows, kv_width), v_buf.dtype)

    for hop in range(1, hops):
        for group in range(key_heads):
            for before, after in zip(copies[hop - 1][group], copies[hop][group]):
                before.wait_recv()
                after.start()
    for copy in local_copies:
        copy.wait()

    factor = math.log2(math.e) / math.sqrt(HEAD_WIDTH)
    own = lax.broadcasted_iota(jnp.int32, (rows, own_rows), 1) <= lax.broadcasted_iota(
        jnp.int32, (rows, own_rows), 0)
    group_width = QUERY_PER_KEY * HEAD_WIDTH
    written = []
    for group in range(key_heads):
        for copy in copies[hops - 1][group]:
            copy.wait_recv()
        columns = slice(group * HEAD_WIDTH, (group + 1) * HEAD_WIDTH)
        at = [group * group_width + i * HEAD_WIDTH for i in range(QUERY_PER_KEY)]
        stacked = jnp.concatenate([q_buf[:, a : a + HEAD_WIDTH] for a in at], axis=0)
        scores = lax.dot_general(
            stacked, k_buf[:, columns], (((1,), (1,)), ((), ())),
            preferred_element_type=jnp.float32)
        weights, inverses = [], []
        for i in range(QUERY_PER_KEY):
            part = scores[i * rows : (i + 1) * rows]
            first = jnp.where(own, part[:, reach:], part[:, :own_rows]) + bias[:, :own_rows]
            rest = part[:, own_rows:reach] + bias[:, own_rows:]
            top = jnp.maximum(
                jnp.max(first, axis=1, keepdims=True), jnp.max(rest, axis=1, keepdims=True)) * factor
            first = jnp.exp2(first * factor - top)
            rest = jnp.exp2(rest * factor - top)
            total = jnp.sum(first, axis=1, keepdims=True) + jnp.sum(rest, axis=1, keepdims=True)
            inverses.append(1.0 / total)
            weights.append(jnp.concatenate(
                [jnp.where(own, 0.0, first).astype(jnp.bfloat16), rest.astype(jnp.bfloat16),
                 jnp.where(own, first, 0.0).astype(jnp.bfloat16)], axis=1))
        summed = jnp.dot(
            jnp.concatenate(weights, axis=0), v_buf[:, columns],
            preferred_element_type=jnp.float32)
        for i in range(QUERY_PER_KEY):
            o_buf[:, at[i] : at[i] + HEAD_WIDTH] = (
                summed[i * rows : (i + 1) * rows] * inverses[i]).astype(o_buf.dtype)
        span = pl.ds(group * group_width, group_width)
        copy = pltpu.make_async_copy(o_buf.at[:, span], o_hbm.at[:, span], out_sem.at[group])
        copy.start()
        written.append(copy)
    for hop in range(hops):
        for group in range(key_heads):
            for copy in copies[hop][group]:
                copy.wait_send()
    for copy in written:
        copy.wait()


def local(sizes, queries, keys, values, doc_lengths):
    rows, kv_width = keys.shape
    key_heads = kv_width // HEAD_WIDTH
    reach = DOCUMENT_SPAN * rows * sizes[2] // 2
    hops = reach // rows
    own_rows = max(rows, LANES)
    spare = -doc_lengths.shape[0] % (8 * LANES)
    lengths = jnp.pad(doc_lengths, (0, spare)).reshape(-1, LANES)
    anywhere = pl.BlockSpec(memory_space=pl.ANY)
    return pl.pallas_call(
        functools.partial(kernel, sizes),
        out_shape=jax.ShapeDtypeStruct(queries.shape, queries.dtype),
        in_specs=[anywhere, anywhere, anywhere, pl.BlockSpec(memory_space=pltpu.VMEM)],
        out_specs=anywhere,
        scratch_shapes=[
            pltpu.VMEM(queries.shape, queries.dtype),
            pltpu.VMEM((reach + own_rows, kv_width), keys.dtype),
            pltpu.VMEM((reach + own_rows, kv_width), values.dtype),
            pltpu.VMEM(queries.shape, queries.dtype),
            pltpu.VMEM((rows, reach), jnp.float32),
            pltpu.SemaphoreType.DMA((hops, key_heads, 2)),
            pltpu.SemaphoreType.DMA((hops, key_heads, 2)),
            pltpu.SemaphoreType.DMA((3,)),
            pltpu.SemaphoreType.DMA((key_heads,)),
        ],
        compiler_params=pltpu.CompilerParams(
            collective_id=0, has_side_effects=True, vmem_limit_bytes=40 * 1024 * 1024),
        name="ring_attention",
    )(queries, keys, values, lengths)


def solution(mesh):
    sizes = (mesh.shape["outer"], mesh.shape["inner"], mesh.shape["head"])
    spread = P(("outer", "inner", "head"), None)
    return jax.shard_map(
        functools.partial(local, sizes),
        mesh=mesh,
        in_specs=(spread, spread, spread, P()),
        out_specs=spread,
        check_vma=False,
    )
```

profile of v0, /device:TPU:0, one launch (start us, length us, event | category | flops | bytes accessed | tf_op | source)
XLA Modules:
  0.0 16.8 jit_solution(6287903523674737188)
XLA Ops:
  0.0 0.7 %pad_bitcast_fusion.len_ref = s32[8,128]{1,0:T(8,128)S(1)} fusion(s32[256]{0:T(256)} %param.7), kind=kLoop, calls=%fused_computation | loop fusion | bytes 5120 | tf_op jit(solution)/shard_map/reshape | solution.py:171
  0.7 0.0 copy-start
  0.7 1.2 %copy-done = bf16[128,4096]{1,0:T(8,128)(2,1)S(1)} copy-done((bf16[128,4096]{1,0:T(8,128)(2,1)S(1)}, bf16[128,4096]{1,0:T(8,128)(2,1)}, u32[]{:S(2)}) %copy-start) | copy-done | bytes 1048600
  1.9 0.0 copy-start.1
  1.9 0.9 %copy-done.1 = bf16[128,512]{1,0:T(8,128)(2,1)S(1)} copy-done((bf16[128,512]{1,0:T(8,128)(2,1)S(1)}, bf16[128,512]{1,0:T(8,128)(2,1)}, u32[]{:S(2)}) %copy-start.1) | copy-done | bytes 131096
  2.8 0.0 copy-start.2
  2.8 0.9 %copy-done.2 = bf16[128,512]{1,0:T(8,128)(2,1)S(1)} copy-done((bf16[128,512]{1,0:T(8,128)(2,1)S(1)}, bf16[128,512]{1,0:T(8,128)(2,1)}, u32[]{:S(2)}) %copy-start.2) | copy-done | bytes 131096
  3.7 12.1 %ring_attention.1 = bf16[128,4096]{1,0:T(8,128)(2,1)S(1)} custom-call(bf16[128,4096]{1,0:T(8,128)(2,1)S(1)} %copy-done, bf16[128,512]{1,0:T(8,128)(2,1)S(1)} %copy-done.1, bf16[128,512]{1,0:T(8,128)(2,1)S(1)} %copy-done.2, s32[8,128]{1,0:T(8,128)S(1)} %pad_bitcast_fusion.len_ref), custom_call_target="tpu_custom_call" | custom-call | tf_op jit(solution)/shard_map/ring_attention/pallas_call | solution.py:173
  15.8 1.0 %copy.6 = bf16[128,4096]{1,0:T(8,128)(2,1)} copy(bf16[128,4096]{1,0:T(8,128)(2,1)S(1)} %ring_attention.1) | data formatting | bytes 2097152
Async XLA Ops:
  0.7 1.2 %copy-start = (bf16[128,4096]{1,0:T(8,128)(2,1)S(1)}, bf16[128,4096]{1,0:T(8,128)(2,1)}, u32[]{:S(2)}) copy-start(bf16[128,4096]{1,0:T(8,128)(2,1)} %q_hbm.1) | copy-start | bytes 3145732
  1.9 0.9 %copy-start.1 = (bf16[128,512]{1,0:T(8,128)(2,1)S(1)}, bf16[128,512]{1,0:T(8,128)(2,1)}, u32[]{:S(2)}) copy-start(bf16[128,512]{1,0:T(8,128)(2,1)} %k_hbm.1) | copy-start | bytes 393220
  2.8 0.9 %copy-start.2 = (bf16[128,512]{1,0:T(8,128)(2,1)S(1)}, bf16[128,512]{1,0:T(8,128)(2,1)}, u32[]{:S(2)}) copy-start(bf16[128,512]{1,0:T(8,128)(2,1)} %v_hbm.1) | copy-start | bytes 393220
where the time goes:
time: 17 us; the launch traced here: 16.8 us
  Pallas kernels  12.1 us (71%)
  local copies, waits for them, and re-layouts  4.69 us (28%)
    pallas_call x1, Pallas kernels, local(): pl.pallas_call(functools.partial(kernel, sizes), out_shape=jax.ShapeDtype...  12.1 us
    unnamed x7, local copies, waits for them, and re-layouts  4 us
    reshape x1, local copies, waits for them, and re-layouts, local(): lengths = jnp.pad(doc_lengths, (0, spare)).reshape(-1, LANES)  0.68 us

commit v1 on v0

--- a/solution.py
+++ b/solution.py
@@ -40,8 +40,8 @@
     return jnp.max(starts, axis=1, keepdims=True)
 
 
-def kernel(sizes, q_hbm, k_hbm, v_hbm, len_ref, o_hbm, q_buf, k_buf, v_buf, o_buf, bias,
-           send_sem, recv_sem, in_sem, out_sem):
+def kernel(sizes, q_hbm, k_hbm, v_hbm, len_hbm, o_buf, q_buf, k_buf, v_buf, len_buf, bias,
+           send_sem, recv_sem, in_sem):
     outer_count, inner_count, head_count = sizes
     rows, kv_width = k_hbm.shape
     key_heads = kv_width // HEAD_WIDTH
@@ -66,9 +66,10 @@
     pl.semaphore_signal(barrier, inc=1, device_id=preceding, device_id_type=pl.DeviceIdType.MESH)
 
     local_copies = [
-        pltpu.make_async_copy(k_hbm, k_buf.at[pl.ds(reach, rows), :], in_sem.at[0]),
-        pltpu.make_async_copy(v_hbm, v_buf.at[pl.ds(reach, rows), :], in_sem.at[1]),
-        pltpu.make_async_copy(q_hbm, q_buf, in_sem.at[2]),
+        pltpu.make_async_copy(len_hbm, len_buf, in_sem.at[0]),
+        pltpu.make_async_copy(k_hbm, k_buf.at[pl.ds(reach, rows), :], in_sem.at[1]),
+        pltpu.make_async_copy(v_hbm, v_buf.at[pl.ds(reach, rows), :], in_sem.at[2]),
+        pltpu.make_async_copy(q_hbm, q_buf, in_sem.at[3]),
     ]
     for copy in local_copies:
         copy.start()
@@ -98,7 +99,8 @@
             copy.start()
 
     position = piece * rows + lax.broadcasted_iota(jnp.int32, (rows, LANES), 0)
-    starts = document_starts(len_ref[...], position)
+    local_copies[0].wait()
+    starts = document_starts(len_buf[...], position)
     row_at = lax.broadcasted_iota(jnp.int32, (rows, reach), 0)
     column_at = lax.broadcasted_iota(jnp.int32, (rows, reach), 1)
     key_position = piece * rows + column_at - jnp.where(column_at <= row_at, 0, reach)
@@ -112,17 +114,16 @@
             for before, after in zip(copies[hop - 1][group], copies[hop][group]):
                 before.wait_recv()
                 after.start()
-    for copy in local_copies:
+    for copy in local_copies[1:]:
         copy.wait()
 
     factor = math.log2(math.e) / math.sqrt(HEAD_WIDTH)
     own = lax.broadcasted_iota(jnp.int32, (rows, own_rows), 1) <= lax.broadcasted_iota(
         jnp.int32, (rows, own_rows), 0)
     group_width = QUERY_PER_KEY * HEAD_WIDTH
-    written = []
     for group in range(key_heads):
-        for copy in copies[hops - 1][group]:
-            copy.wait_recv()
+        key_copy, value_copy = copies[hops - 1][group]
+        key_copy.wait_recv()
         columns = slice(group * HEAD_WIDTH, (group + 1) * HEAD_WIDTH)
         at = [group * group_width + i * HEAD_WIDTH for i in range(QUERY_PER_KEY)]
         stacked = jnp.concatenate([q_buf[:, a : a + HEAD_WIDTH] for a in at], axis=0)
@@ -143,22 +144,17 @@
             weights.append(jnp.concatenate(
                 [jnp.where(own, 0.0, first).astype(jnp.bfloat16), rest.astype(jnp.bfloat16),
                  jnp.where(own, first, 0.0).astype(jnp.bfloat16)], axis=1))
+        value_copy.wait_recv()
         summed = jnp.dot(
             jnp.concatenate(weights, axis=0), v_buf[:, columns],
             preferred_element_type=jnp.float32)
         for i in range(QUERY_PER_KEY):
             o_buf[:, at[i] : at[i] + HEAD_WIDTH] = (
                 summed[i * rows : (i + 1) * rows] * inverses[i]).astype(o_buf.dtype)
-        span = pl.ds(group * group_width, group_width)
-        copy = pltpu.make_async_copy(o_buf.at[:, span], o_hbm.at[:, span], out_sem.at[group])
-        copy.start()
-        written.append(copy)
     for hop in range(hops):
         for group in range(key_heads):
             for copy in copies[hop][group]:
                 copy.wait_send()
-    for copy in written:
-        copy.wait()
 
 
 def local(sizes, queries, keys, values, doc_lengths):
@@ -167,29 +163,31 @@
     reach = DOCUMENT_SPAN * rows * sizes[2] // 2
     hops = reach // rows
     own_rows = max(rows, LANES)
-    spare = -doc_lengths.shape[0] % (8 * LANES)
-    lengths = jnp.pad(doc_lengths, (0, spare)).reshape(-1, LANES)
-    anywhere = pl.BlockSpec(memory_space=pl.ANY)
+    lengths = jnp.pad(doc_lengths, (0, -doc_lengths.shape[0] % LANES)).reshape(-1, LANES)
+    operands = [
+        pltpu.with_memory_space_constraint(value, pltpu.HBM)
+        for value in (queries, keys, values, lengths)
+    ]
+    in_hbm = pl.BlockSpec(memory_space=pltpu.HBM)
     return pl.pallas_call(
         functools.partial(kernel, sizes),
-        out_shape=jax.ShapeDtypeStruct(queries.shape, queries.dtype),
-        in_specs=[anywhere, anywhere, anywhere, pl.BlockSpec(memory_space=pltpu.VMEM)],
-        out_specs=anywhere,
+        out_shape=pltpu.VMEM(queries.shape, queries.dtype),
+        in_specs=[in_hbm, in_hbm, in_hbm, in_hbm],
+        out_specs=pl.BlockSpec(memory_space=pltpu.VMEM),
         scratch_shapes=[
             pltpu.VMEM(queries.shape, queries.dtype),
             pltpu.VMEM((reach + own_rows, kv_width), keys.dtype),
             pltpu.VMEM((reach + own_rows, kv_width), values.dtype),
-            pltpu.VMEM(queries.shape, queries.dtype),
+            pltpu.VMEM(lengths.shape, lengths.dtype),
             pltpu.VMEM((rows, reach), jnp.float32),
             pltpu.SemaphoreType.DMA((hops, key_heads, 2)),
             pltpu.SemaphoreType.DMA((hops, key_heads, 2)),
-            pltpu.SemaphoreType.DMA((3,)),
-            pltpu.SemaphoreType.DMA((key_heads,)),
+            pltpu.SemaphoreType.DMA((4,)),
         ],
         compiler_params=pltpu.CompilerParams(
             collective_id=0, has_side_effects=True, vmem_limit_bytes=40 * 1024 * 1024),
         name="ring_attention",
-    )(queries, keys, values, lengths)
+    )(*operands)
 
 
 def solution(mesh):

time: 17 us -> 14.7 us (0.86)
  local copies, waits for them, and re-layouts: 4.69 us -> 0.97 us
  Pallas kernels: 12.1 us -> 13.6 us
    unnamed x7 -> x1, local copies, waits for them, and re-layouts: 4 us -> 0.97 us
    pallas_call x1, Pallas kernels: 12.1 us -> 13.6 us  [local(): pl.pallas_call(functools.partial(kernel, sizes), out_shape=pltpu.VMEM(que...]
    reshape x1 -> x0, local copies, waits for them, and re-layouts: 0.68 us -> none  [local(): lengths = jnp.pad(doc_lengths, (0, spare)).reshape(-1, LANES)]
where the time goes in v1:
time: 14.7 us; the launch traced here: 14.6 us
  Pallas kernels  13.6 us (93%)
  local copies, waits for them, and re-layouts  0.97 us (7%)
    pallas_call x1, Pallas kernels, local(): pl.pallas_call(functools.partial(kernel, sizes), out_shape=pltpu.VMEM(que...  13.6 us
    unnamed x1, local copies, waits for them, and re-layouts  0.97 us

profile of v1, /device:TPU:0, one launch (start us, length us, event | category | flops | bytes accessed | tf_op | source)
XLA Modules:
  0.0 14.6 jit_solution(11230229022008127117)
XLA Ops:
  0.0 13.6 %ring_attention.1 = bf16[128,4096]{1,0:T(8,128)(2,1)S(1)} custom-call(bf16[128,4096]{1,0:T(8,128)(2,1)} %q_hbm.1, bf16[128,512]{1,0:T(8,128)(2,1)} %k_hbm.1, bf16[128,512]{1,0:T(8,128)(2,1)} %v_hbm.1, s32[2,128]{1,0:T(2,128)} %bitcast.1), custom_call_target="tpu_custom_call" | custom-call | tf_op jit(solution)/shard_map/ring_attention/pallas_call | solution.py:172
  13.6 1.0 %copy.6 = bf16[128,4096]{1,0:T(8,128)(2,1)} copy(bf16[128,4096]{1,0:T(8,128)(2,1)S(1)} %ring_attention.1) | data formatting | bytes 2097152

commit v2 on v1

--- a/solution.py
+++ b/solution.py
@@ -50,7 +50,7 @@
     reach = DOCUMENT_SPAN * rows * per_block
     hops = reach // rows
     pieces = contexts * head_count
-    own_rows = k_buf.shape[0] - reach
+    own_rows = k_buf.shape[1] - reach
 
     context = lax.axis_index("outer") * inner_count + lax.axis_index("inner")
     head = lax.axis_index("head")
@@ -65,92 +65,99 @@
     barrier = pltpu.get_barrier_semaphore()
     pl.semaphore_signal(barrier, inc=1, device_id=preceding, device_id_type=pl.DeviceIdType.MESH)
 
-    local_copies = [
-        pltpu.make_async_copy(len_hbm, len_buf, in_sem.at[0]),
-        pltpu.make_async_copy(k_hbm, k_buf.at[pl.ds(reach, rows), :], in_sem.at[1]),
-        pltpu.make_async_copy(v_hbm, v_buf.at[pl.ds(reach, rows), :], in_sem.at[2]),
-        pltpu.make_async_copy(q_hbm, q_buf, in_sem.at[3]),
-    ]
-    for copy in local_copies:
-        copy.start()
+    own_slot = pl.ds(reach, rows)
+    length_copy = pltpu.make_async_copy(len_hbm, len_buf, in_sem.at[0])
+    length_copy.start()
+    held_copies = []
+    for group in range(key_heads):
+        columns = pl.ds(group * HEAD_WIDTH, HEAD_WIDTH)
+        held_copies.append([
+            pltpu.make_async_copy(
+                hbm.at[:, columns], buf.at[group, own_slot, :], in_sem.at[2 + 2 * group + at])
+            for at, (hbm, buf) in enumerate(((k_hbm, k_buf), (v_hbm, v_buf)))
+        ])
+        for copy in held_copies[group]:
+            copy.start()
+    query_copy = pltpu.make_async_copy(q_hbm, q_buf, in_sem.at[1])
+    query_copy.start()
 
     def passing(hop, group):
-        columns = pl.ds(group * HEAD_WIDTH, HEAD_WIDTH)
-        found = []
-        for at, (hbm, buf) in enumerate(((k_hbm, k_buf), (v_hbm, v_buf))):
-            if hop == 0:
-                source = hbm.at[:, columns]
-            else:
-                source = buf.at[pl.ds(reach - hop * rows, rows), columns]
-            found.append(pltpu.make_async_remote_copy(
-                src_ref=source,
-                dst_ref=buf.at[pl.ds(reach - (hop + 1) * rows, rows), columns],
+        return [
+            pltpu.make_async_remote_copy(
+                src_ref=buf.at[group, pl.ds(reach - hop * rows, rows), :],
+                dst_ref=buf.at[group, pl.ds(reach - (hop + 1) * rows, rows), :],
                 send_sem=send_sem.at[hop, group, at],
                 recv_sem=recv_sem.at[hop, group, at],
                 device_id=following,
                 device_id_type=pl.DeviceIdType.MESH,
-            ))
-        return found
+            )
+            for at, buf in enumerate((k_buf, v_buf))
+        ]
 
     copies = [[passing(hop, group) for group in range(key_heads)] for hop in range(hops)]
-    pl.semaphore_wait(barrier, 1)
-    for group in range(key_heads):
-        for copy in copies[0][group]:
-            copy.start()
-
+
+    length_copy.wait()
     position = piece * rows + lax.broadcasted_iota(jnp.int32, (rows, LANES), 0)
-    local_copies[0].wait()
     starts = document_starts(len_buf[...], position)
     row_at = lax.broadcasted_iota(jnp.int32, (rows, reach), 0)
     column_at = lax.broadcasted_iota(jnp.int32, (rows, reach), 1)
     key_position = piece * rows + column_at - jnp.where(column_at <= row_at, 0, reach)
     bias[...] = jnp.where(key_position >= starts, 0.0, NEG)
     if own_rows > rows:
-        k_buf[reach + rows :, :] = jnp.zeros((own_rows - rows, kv_width), k_buf.dtype)
-        v_buf[reach + rows :, :] = jnp.zeros((own_rows - rows, kv_width), v_buf.dtype)
-
-    for hop in range(1, hops):
-        for group in range(key_heads):
-            for before, after in zip(copies[hop - 1][group], copies[hop][group]):
-                before.wait_recv()
-                after.start()
-    for copy in local_copies[1:]:
-        copy.wait()
+        blank = jnp.zeros((key_heads, own_rows - rows, HEAD_WIDTH), k_buf.dtype)
+        k_buf[:, reach + rows :, :] = blank
+        v_buf[:, reach + rows :, :] = blank
+    for pair in held_copies:
+        for copy in pair:
+            copy.wait()
+    pl.semaphore_wait(barrier, 1)
 
     factor = math.log2(math.e) / math.sqrt(HEAD_WIDTH)
     own = lax.broadcasted_iota(jnp.int32, (rows, own_rows), 1) <= lax.broadcasted_iota(
         jnp.int32, (rows, own_rows), 0)
     group_width = QUERY_PER_KEY * HEAD_WIDTH
-    for group in range(key_heads):
+
+    def send(hop, group):
+        for at, copy in enumerate(copies[hop][group]):
+            if hop > 0:
+                copies[hop - 1][group][at].wait_recv()
+            copy.start()
+
+    def attend(group):
+        if group == 0:
+            query_copy.wait()
+        at = [group * group_width + i * HEAD_WIDTH for i in range(QUERY_PER_KEY)]
+        stacked = jnp.concatenate([q_buf[:, a : a + HEAD_WIDTH] for a in at], axis=0)
         key_copy, value_copy = copies[hops - 1][group]
         key_copy.wait_recv()
-        columns = slice(group * HEAD_WIDTH, (group + 1) * HEAD_WIDTH)
-        at = [group * group_width + i * HEAD_WIDTH for i in range(QUERY_PER_KEY)]
-        stacked = jnp.concatenate([q_buf[:, a : a + HEAD_WIDTH] for a in at], axis=0)
         scores = lax.dot_general(
-            stacked, k_buf[:, columns], (((1,), (1,)), ((), ())),
-            preferred_element_type=jnp.float32)
+            stacked, k_buf[group], (((1,), (1,)), ((), ())), preferred_element_type=jnp.float32)
         weights, inverses = [], []
         for i in range(QUERY_PER_KEY):
             part = scores[i * rows : (i + 1) * rows]
             first = jnp.where(own, part[:, reach:], part[:, :own_rows]) + bias[:, :own_rows]
             rest = part[:, own_rows:reach] + bias[:, own_rows:]
-            top = jnp.maximum(
-                jnp.max(first, axis=1, keepdims=True), jnp.max(rest, axis=1, keepdims=True)) * factor
+            top = jnp.max(jnp.maximum(first, rest), axis=1, keepdims=True) * factor
             first = jnp.exp2(first * factor - top)
             rest = jnp.exp2(rest * factor - top)
-            total = jnp.sum(first, axis=1, keepdims=True) + jnp.sum(rest, axis=1, keepdims=True)
-            inverses.append(1.0 / total)
+            inverses.append(1.0 / jnp.sum(first + rest, axis=1, keepdims=True))
             weights.append(jnp.concatenate(
                 [jnp.where(own, 0.0, first).astype(jnp.bfloat16), rest.astype(jnp.bfloat16),
                  jnp.where(own, first, 0.0).astype(jnp.bfloat16)], axis=1))
         value_copy.wait_recv()
         summed = jnp.dot(
-            jnp.concatenate(weights, axis=0), v_buf[:, columns],
-            preferred_element_type=jnp.float32)
+            jnp.concatenate(weights, axis=0), v_buf[group], preferred_element_type=jnp.float32)
         for i in range(QUERY_PER_KEY):
             o_buf[:, at[i] : at[i] + HEAD_WIDTH] = (
                 summed[i * rows : (i + 1) * rows] * inverses[i]).astype(o_buf.dtype)
+
+    events = []
+    for group in range(key_heads):
+        for hop in range(hops):
+            events.append((20 * group + 30 * hop, functools.partial(send, hop, group)))
+        events.append((20 * group + 30 * hops + 2, functools.partial(attend, group)))
+    for _, event in sorted(events, key=lambda pair: pair[0]):
+        event()
     for hop in range(hops):
         for group in range(key_heads):
             for copy in copies[hop][group]:
@@ -176,13 +183,13 @@
         out_specs=pl.BlockSpec(memory_space=pltpu.VMEM),
         scratch_shapes=[
             pltpu.VMEM(queries.shape, queries.dtype),
-            pltpu.VMEM((reach + own_rows, kv_width), keys.dtype),
-            pltpu.VMEM((reach + own_rows, kv_width), values.dtype),
+            pltpu.VMEM((key_heads, reach + own_rows, HEAD_WIDTH), keys.dtype),
+            pltpu.VMEM((key_heads, reach + own_rows, HEAD_WIDTH), values.dtype),
             pltpu.VMEM(lengths.shape, lengths.dtype),
             pltpu.VMEM((rows, reach), jnp.float32),
             pltpu.SemaphoreType.DMA((hops, key_heads, 2)),
             pltpu.SemaphoreType.DMA((hops, key_heads, 2)),
-            pltpu.SemaphoreType.DMA((4,)),
+            pltpu.SemaphoreType.DMA((2 + 2 * key_heads,)),
         ],
         compiler_params=pltpu.CompilerParams(
             collective_id=0, has_side_effects=True, vmem_limit_bytes=40 * 1024 * 1024),

time: 14.7 us -> 14.9 us (1.014)
  no operation moved by 1% of the time
where the time goes in v2:
time: 14.9 us; the launch traced here: 14.7 us
  Pallas kernels  13.7 us (92%)
  local copies, waits for them, and re-layouts  0.97 us (7%)
    pallas_call x1, Pallas kernels, local(): pl.pallas_call(functools.partial(kernel, sizes), out_shape=pltpu.VMEM(que...  13.7 us
    unnamed x1, local copies, waits for them, and re-layouts  0.97 us

profile of v2, /device:TPU:0, one launch (start us, length us, event | category | flops | bytes accessed | tf_op | source)
XLA Modules:
  0.0 14.7 jit_solution(15260369455507589054)
XLA Ops:
  0.0 13.7 %ring_attention.1 = bf16[128,4096]{1,0:T(8,128)(2,1)S(1)} custom-call(bf16[128,4096]{1,0:T(8,128)(2,1)} %q_hbm.1, bf16[128,512]{1,0:T(8,128)(2,1)} %k_hbm.1, bf16[128,512]{1,0:T(8,128)(2,1)} %v_hbm.1, s32[2,128]{1,0:T(2,128)} %bitcast.1), custom_call_target="tpu_custom_call" | custom-call | tf_op jit(solution)/shard_map/ring_attention/pallas_call | solution.py:179
  13.8 1.0 %copy.6 = bf16[128,4096]{1,0:T(8,128)(2,1)} copy(bf16[128,4096]{1,0:T(8,128)(2,1)S(1)} %ring_attention.1) | data formatting | bytes 2097152

commit v3 on v2

--- a/solution.py
+++ b/solution.py
@@ -62,8 +62,19 @@
     following = place(lax.rem(piece + 1, pieces))
     preceding = place(lax.rem(piece + pieces - 1, pieces))
 
+    paired = hops == 2
+    lead = lax.rem(piece, 2) == 0
+
     barrier = pltpu.get_barrier_semaphore()
     pl.semaphore_signal(barrier, inc=1, device_id=preceding, device_id_type=pl.DeviceIdType.MESH)
+    if paired:
+        after_next = place(lax.rem(piece + 2, pieces))
+        before_last = place(lax.rem(piece + pieces - 2, pieces))
+
+        @pl.when(lead)
+        def _():
+            pl.semaphore_signal(
+                barrier, inc=1, device_id=before_last, device_id_type=pl.DeviceIdType.MESH)
 
     own_slot = pl.ds(reach, rows)
     length_copy = pltpu.make_async_copy(len_hbm, len_buf, in_sem.at[0])
@@ -96,6 +107,19 @@
 
     copies = [[passing(hop, group) for group in range(key_heads)] for hop in range(hops)]
 
+    def skipping(group):
+        return [
+            pltpu.make_async_remote_copy(
+                src_ref=buf.at[group, own_slot, :],
+                dst_ref=buf.at[group, pl.ds(reach - 2 * rows, rows), :],
+                send_sem=send_sem.at[hops, group, at],
+                recv_sem=recv_sem.at[1, group, at],
+                device_id=after_next,
+                device_id_type=pl.DeviceIdType.MESH,
+            )
+            for at, buf in enumerate((k_buf, v_buf))
+        ]
+
     length_copy.wait()
     position = piece * rows + lax.broadcasted_iota(jnp.int32, (rows, LANES), 0)
     starts = document_starts(len_buf[...], position)
@@ -110,7 +134,17 @@
     for pair in held_copies:
         for copy in pair:
             copy.wait()
-    pl.semaphore_wait(barrier, 1)
+    pl.semaphore_wait(barrier, jnp.where(lead, 2, 1) if paired else 1)
+    if paired:
+        @pl.when(lead)
+        def _():
+            for group in range(key_heads):
+                for copy in skipping(group):
+                    copy.start()
+
+        for group in range(key_heads):
+            for copy in copies[0][group]:
+                copy.start()
 
     factor = math.log2(math.e) / math.sqrt(HEAD_WIDTH)
     own = lax.broadcasted_iota(jnp.int32, (rows, own_rows), 1) <= lax.broadcasted_iota(
@@ -121,7 +155,10 @@
         for at, copy in enumerate(copies[hop][group]):
             if hop > 0:
                 copies[hop - 1][group][at].wait_recv()
-            copy.start()
+            if paired:
+                pl.when(lead)(copy.start)
+            else:
+                copy.start()
 
     def attend(group):
         if group == 0:
@@ -153,15 +190,21 @@
 
     events = []
     for group in range(key_heads):
-        for hop in range(hops):
+        for hop in range(1 if paired else 0, hops):
             events.append((20 * group + 30 * hop, functools.partial(send, hop, group)))
         events.append((20 * group + 30 * hops + 2, functools.partial(attend, group)))
     for _, event in sorted(events, key=lambda pair: pair[0]):
         event()
-    for hop in range(hops):
+    for hop in range(1 if paired else hops):
         for group in range(key_heads):
             for copy in copies[hop][group]:
                 copy.wait_send()
+    if paired:
+        @pl.when(lead)
+        def _():
+            for group in range(key_heads):
+                for copy in copies[1][group] + skipping(group):
+                    copy.wait_send()
 
 
 def local(sizes, queries, keys, values, doc_lengths):
@@ -187,7 +230,7 @@
             pltpu.VMEM((key_heads, reach + own_rows, HEAD_WIDTH), values.dtype),
             pltpu.VMEM(lengths.shape, lengths.dtype),
             pltpu.VMEM((rows, reach), jnp.float32),
-            pltpu.SemaphoreType.DMA((hops, key_heads, 2)),
+            pltpu.SemaphoreType.DMA((hops + 1, key_heads, 2)),
             pltpu.SemaphoreType.DMA((hops, key_heads, 2)),
             pltpu.SemaphoreType.DMA((2 + 2 * key_heads,)),
         ],

time: 14.9 us -> 14.8 us (level)
  no operation moved by 1% of the time
where the time goes in v3:
time: 14.8 us; the launch traced here: 14.7 us
  Pallas kernels  13.7 us (93%)
  local copies, waits for them, and re-layouts  0.97 us (7%)
    pallas_call x1, Pallas kernels, local(): pl.pallas_call(functools.partial(kernel, sizes), out_shape=pltpu.VMEM(que...  13.7 us
    unnamed x1, local copies, waits for them, and re-layouts  0.97 us

profile of v3, /device:TPU:0, one launch (start us, length us, event | category | flops | bytes accessed | tf_op | source)
XLA Modules:
  0.0 14.7 jit_solution(14148075431198040242)
XLA Ops:
  0.0 13.7 %ring_attention.1 = bf16[128,4096]{1,0:T(8,128)(2,1)S(1)} custom-call(bf16[128,4096]{1,0:T(8,128)(2,1)} %q_hbm.1, bf16[128,512]{1,0:T(8,128)(2,1)} %k_hbm.1, bf16[128,512]{1,0:T(8,128)(2,1)} %v_hbm.1, s32[2,128]{1,0:T(2,128)} %bitcast.1), custom_call_target="tpu_custom_call" | custom-call | tf_op jit(solution)/shard_map/ring_attention/pallas_call | solution.py:222
  13.7 1.0 %copy.6 = bf16[128,4096]{1,0:T(8,128)(2,1)} copy(bf16[128,4096]{1,0:T(8,128)(2,1)S(1)} %ring_attention.1) | data formatting | bytes 2097152

commit v4 on v3

--- a/solution.py
+++ b/solution.py
@@ -66,15 +66,19 @@
     lead = lax.rem(piece, 2) == 0
 
     barrier = pltpu.get_barrier_semaphore()
-    pl.semaphore_signal(barrier, inc=1, device_id=preceding, device_id_type=pl.DeviceIdType.MESH)
+
+    def greet(device):
+        pl.semaphore_signal(barrier, inc=1, device_id=device, device_id_type=pl.DeviceIdType.MESH)
+
+    has_next = piece + 1 < pieces
+    peers = jnp.where(has_next, 1, 0)
+    pl.when(piece >= 1)(functools.partial(greet, preceding))
     if paired:
         after_next = place(lax.rem(piece + 2, pieces))
         before_last = place(lax.rem(piece + pieces - 2, pieces))
-
-        @pl.when(lead)
-        def _():
-            pl.semaphore_signal(
-                barrier, inc=1, device_id=before_last, device_id_type=pl.DeviceIdType.MESH)
+        has_second = jnp.logical_and(lead, piece + 2 < pieces)
+        peers = peers + jnp.where(has_second, 1, 0)
+        pl.when(jnp.logical_and(lead, piece >= 2))(functools.partial(greet, before_last))
 
     own_slot = pl.ds(reach, rows)
     length_copy = pltpu.make_async_copy(len_hbm, len_buf, in_sem.at[0])
@@ -131,42 +135,52 @@
         blank = jnp.zeros((key_heads, own_rows - rows, HEAD_WIDTH), k_buf.dtype)
         k_buf[:, reach + rows :, :] = blank
         v_buf[:, reach + rows :, :] = blank
+    for distance in range(1, hops + 1):
+        @pl.when(piece < distance)
+        def _():
+            blank = jnp.zeros((key_heads, rows, HEAD_WIDTH), k_buf.dtype)
+            k_buf[:, reach - distance * rows : reach - (distance - 1) * rows, :] = blank
+            v_buf[:, reach - distance * rows : reach - (distance - 1) * rows, :] = blank
+
     for pair in held_copies:
         for copy in pair:
             copy.wait()
-    pl.semaphore_wait(barrier, jnp.where(lead, 2, 1) if paired else 1)
+    pl.when(has_next)(lambda: pl.semaphore_wait(barrier, peers))
+
+    def start_all(found):
+        for copy in found:
+            copy.start()
+
+    def wait_sent(found):
+        for copy in found:
+            copy.wait_send()
+
     if paired:
-        @pl.when(lead)
-        def _():
-            for group in range(key_heads):
-                for copy in skipping(group):
-                    copy.start()
-
         for group in range(key_heads):
-            for copy in copies[0][group]:
-                copy.start()
+            pl.when(has_second)(functools.partial(start_all, skipping(group)))
+            pl.when(has_next)(functools.partial(start_all, copies[0][group]))
 
     factor = math.log2(math.e) / math.sqrt(HEAD_WIDTH)
     own = lax.broadcasted_iota(jnp.int32, (rows, own_rows), 1) <= lax.broadcasted_iota(
         jnp.int32, (rows, own_rows), 0)
     group_width = QUERY_PER_KEY * HEAD_WIDTH
 
+    def sends(hop):
+        there = jnp.logical_and(has_next, piece >= hop)
+        return jnp.logical_and(there, lead) if paired and hop > 0 else there
+
     def send(hop, group):
         for at, copy in enumerate(copies[hop][group]):
             if hop > 0:
-                copies[hop - 1][group][at].wait_recv()
-            if paired:
-                pl.when(lead)(copy.start)
-            else:
-                copy.start()
-
-    def attend(group):
-        if group == 0:
-            query_copy.wait()
-        at = [group * group_width + i * HEAD_WIDTH for i in range(QUERY_PER_KEY)]
-        stacked = jnp.concatenate([q_buf[:, a : a + HEAD_WIDTH] for a in at], axis=0)
-        key_copy, value_copy = copies[hops - 1][group]
-        key_copy.wait_recv()
+                pl.when(piece >= hop)(copies[hop - 1][group][at].wait_recv)
+            pl.when(sends(hop))(copy.start)
+
+    def columns_of(group):
+        return [group * group_width + i * HEAD_WIDTH for i in range(QUERY_PER_KEY)]
+
+    def weigh(group):
+        stacked = jnp.concatenate(
+            [q_buf[:, a : a + HEAD_WIDTH] for a in columns_of(group)], axis=0)
         scores = lax.dot_general(
             stacked, k_buf[group], (((1,), (1,)), ((), ())), preferred_element_type=jnp.float32)
         weights, inverses = [], []
@@ -177,34 +191,47 @@
             top = jnp.max(jnp.maximum(first, rest), axis=1, keepdims=True) * factor
             first = jnp.exp2(first * factor - top)
             rest = jnp.exp2(rest * factor - top)
-            inverses.append(1.0 / jnp.sum(first + rest, axis=1, keepdims=True))
+            total = jnp.sum(first + rest, axis=1, keepdims=True)
+            estimate = pl.reciprocal(total, approx=True)
+            inverses.append(estimate * (2.0 - total * estimate))
             weights.append(jnp.concatenate(
                 [jnp.where(own, 0.0, first).astype(jnp.bfloat16), rest.astype(jnp.bfloat16),
                  jnp.where(own, first, 0.0).astype(jnp.bfloat16)], axis=1))
-        value_copy.wait_recv()
-        summed = jnp.dot(
-            jnp.concatenate(weights, axis=0), v_buf[group], preferred_element_type=jnp.float32)
-        for i in range(QUERY_PER_KEY):
-            o_buf[:, at[i] : at[i] + HEAD_WIDTH] = (
+        return jnp.concatenate(weights, axis=0), inverses
+
+    def gather(group, weights, inverses):
+        summed = jnp.dot(weights, v_buf[group], preferred_element_type=jnp.float32)
+        for i, a in enumerate(columns_of(group)):
+            o_buf[:, a : a + HEAD_WIDTH] = (
                 summed[i * rows : (i + 1) * rows] * inverses[i]).astype(o_buf.dtype)
 
+    held = []
+
+    def attend(group):
+        if group == 0:
+            query_copy.wait()
+        else:
+            pl.when(piece >= hops)(copies[hops - 1][group - 1][1].wait_recv)
+        if group < key_heads:
+            pl.when(piece >= hops)(copies[hops - 1][group][0].wait_recv)
+        if group > 0:
+            gather(group - 1, *held.pop())
+        if group < key_heads:
+            held.append(weigh(group))
+
     events = []
-    for group in range(key_heads):
-        for hop in range(1 if paired else 0, hops):
-            events.append((20 * group + 30 * hop, functools.partial(send, hop, group)))
+    for group in range(key_heads + 1):
+        if group < key_heads:
+            for hop in range(1 if paired else 0, hops):
+                events.append((20 * group + 30 * hop, functools.partial(send, hop, group)))
         events.append((20 * group + 30 * hops + 2, functools.partial(attend, group)))
     for _, event in sorted(events, key=lambda pair: pair[0]):
         event()
-    for hop in range(1 if paired else hops):
-        for group in range(key_heads):
-            for copy in copies[hop][group]:
-                copy.wait_send()
-    if paired:
-        @pl.when(lead)
-        def _():
-            for group in range(key_heads):
-                for copy in copies[1][group] + skipping(group):
-                    copy.wait_send()
+    for group in range(key_heads):
+        for hop in range(hops):
+            pl.when(sends(hop))(functools.partial(wait_sent, copies[hop][group]))
+        if paired:
+            pl.when(has_second)(functools.partial(wait_sent, skipping(group)))
 
 
 def local(sizes, queries, keys, values, doc_lengths):

time: 14.8 us -> 13.1 us (0.89)
  the two profiles are of different devices: /device:TPU:0 before, /device:TPU:29 now
where the time goes in v4:
time: 13.1 us; the launch traced here: 12.9 us
  Pallas kernels  11.9 us (91%)
  local copies, waits for them, and re-layouts  0.97 us (7%)
    pallas_call x1, Pallas kernels, local(): pl.pallas_call(functools.partial(kernel, sizes), out_shape=pltpu.VMEM(que...  11.9 us
    unnamed x1, local copies, waits for them, and re-layouts  0.97 us

profile of v4, /device:TPU:29, one launch (start us, length us, event | category | flops | bytes accessed | tf_op | source)
XLA Modules:
  0.0 12.9 jit_solution(9430494803009025607)
XLA Ops:
  0.0 11.9 %ring_attention.1 = bf16[128,4096]{1,0:T(8,128)(2,1)S(1)} custom-call(bf16[128,4096]{1,0:T(8,128)(2,1)} %q_hbm.1, bf16[128,512]{1,0:T(8,128)(2,1)} %k_hbm.1, bf16[128,512]{1,0:T(8,128)(2,1)} %v_hbm.1, s32[2,128]{1,0:T(2,128)} %bitcast.1), custom_call_target="tpu_custom_call" | custom-call | tf_op jit(solution)/shard_map/ring_attention/pallas_call | solution.py:249
  11.9 1.0 %copy.6 = bf16[128,4096]{1,0:T(8,128)(2,1)} copy(bf16[128,4096]{1,0:T(8,128)(2,1)S(1)} %ring_attention.1) | data formatting | bytes 2097152

commit v5 on v4

--- a/solution.py
+++ b/solution.py
@@ -32,12 +32,15 @@
         within = within + jnp.where(lane >= step, pltpu.roll(within, step, 1), 0)
         step *= 2
     before = jnp.zeros((1, 1), jnp.int32)
-    starts = jnp.zeros(positions.shape, jnp.int32)
+    starts = jnp.zeros((1, LANES), jnp.float32)
     for row in range(lengths.shape[0]):
         ends = before + within[row : row + 1, :]
-        starts = jnp.maximum(starts, jnp.where(ends <= positions, ends, 0))
+        spread = jnp.transpose(
+            jnp.broadcast_to(ends.astype(jnp.float32), (LANES, LANES)))
+        passed = jnp.where(spread <= positions, spread, 0.0)
+        starts = jnp.maximum(starts, jnp.max(passed, axis=0, keepdims=True))
         before = ends[:, LANES - 1 :]
-    return jnp.max(starts, axis=1, keepdims=True)
+    return starts
 
 
 def kernel(sizes, q_hbm, k_hbm, v_hbm, len_hbm, o_buf, q_buf, k_buf, v_buf, len_buf, bias,
@@ -125,12 +128,12 @@
         ]
 
     length_copy.wait()
-    position = piece * rows + lax.broadcasted_iota(jnp.int32, (rows, LANES), 0)
-    starts = document_starts(len_buf[...], position)
-    row_at = lax.broadcasted_iota(jnp.int32, (rows, reach), 0)
-    column_at = lax.broadcasted_iota(jnp.int32, (rows, reach), 1)
-    key_position = piece * rows + column_at - jnp.where(column_at <= row_at, 0, reach)
-    bias[...] = jnp.where(key_position >= starts, 0.0, NEG)
+    lane_at = lax.rem(lax.broadcasted_iota(jnp.int32, (LANES, LANES), 1), rows)
+    starts = document_starts(len_buf[...], (piece * rows + lane_at).astype(jnp.float32))
+    key_at = lax.broadcasted_iota(jnp.int32, (reach, LANES), 0)
+    query_at = lax.rem(lax.broadcasted_iota(jnp.int32, (reach, LANES), 1), rows)
+    key_position = piece * rows + key_at - jnp.where(key_at <= query_at, 0, reach)
+    bias[...] = jnp.where(key_position.astype(jnp.float32) >= starts, 0.0, NEG)
     if own_rows > rows:
         blank = jnp.zeros((key_heads, own_rows - rows, HEAD_WIDTH), k_buf.dtype)
         k_buf[:, reach + rows :, :] = blank
@@ -161,8 +164,9 @@
             pl.when(has_next)(functools.partial(start_all, copies[0][group]))
 
     factor = math.log2(math.e) / math.sqrt(HEAD_WIDTH)
-    own = lax.broadcasted_iota(jnp.int32, (rows, own_rows), 1) <= lax.broadcasted_iota(
-        jnp.int32, (rows, own_rows), 0)
+    own = lax.broadcasted_iota(jnp.int32, (own_rows, LANES), 0) <= lax.rem(
+        lax.broadcasted_iota(jnp.int32, (own_rows, LANES), 1), rows)
+    chunks = QUERY_PER_KEY * rows // LANES
     group_width = QUERY_PER_KEY * HEAD_WIDTH
 
     def sends(hop):
@@ -182,28 +186,31 @@
         stacked = jnp.concatenate(
             [q_buf[:, a : a + HEAD_WIDTH] for a in columns_of(group)], axis=0)
         scores = lax.dot_general(
-            stacked, k_buf[group], (((1,), (1,)), ((), ())), preferred_element_type=jnp.float32)
+            k_buf[group], stacked, (((1,), (1,)), ((), ())), preferred_element_type=jnp.float32)
         weights, inverses = [], []
-        for i in range(QUERY_PER_KEY):
-            part = scores[i * rows : (i + 1) * rows]
-            first = jnp.where(own, part[:, reach:], part[:, :own_rows]) + bias[:, :own_rows]
-            rest = part[:, own_rows:reach] + bias[:, own_rows:]
-            top = jnp.max(jnp.maximum(first, rest), axis=1, keepdims=True) * factor
+        for i in range(chunks):
+            part = scores[:, i * LANES : (i + 1) * LANES]
+            first = jnp.where(own, part[reach:], part[:own_rows]) + bias[:own_rows, :]
+            rest = part[own_rows:reach] + bias[own_rows:, :]
+            top = jnp.max(jnp.maximum(first, rest), axis=0, keepdims=True) * factor
             first = jnp.exp2(first * factor - top)
             rest = jnp.exp2(rest * factor - top)
-            total = jnp.sum(first + rest, axis=1, keepdims=True)
-            estimate = pl.reciprocal(total, approx=True)
-            inverses.append(estimate * (2.0 - total * estimate))
+            inverses.append(1.0 / jnp.sum(first + rest, axis=0, keepdims=True))
             weights.append(jnp.concatenate(
                 [jnp.where(own, 0.0, first).astype(jnp.bfloat16), rest.astype(jnp.bfloat16),
-                 jnp.where(own, first, 0.0).astype(jnp.bfloat16)], axis=1))
-        return jnp.concatenate(weights, axis=0), inverses
+                 jnp.where(own, first, 0.0).astype(jnp.bfloat16)], axis=0))
+        return jnp.concatenate(weights, axis=1), inverses
 
     def gather(group, weights, inverses):
-        summed = jnp.dot(weights, v_buf[group], preferred_element_type=jnp.float32)
-        for i, a in enumerate(columns_of(group)):
-            o_buf[:, a : a + HEAD_WIDTH] = (
-                summed[i * rows : (i + 1) * rows] * inverses[i]).astype(o_buf.dtype)
+        summed = jnp.dot(
+            jnp.transpose(v_buf[group]), weights, preferred_element_type=jnp.float32)
+        columns = columns_of(group)
+        for i in range(chunks):
+            part = summed[:, i * LANES : (i + 1) * LANES] * inverses[i]
+            turned = jnp.transpose(part).astype(o_buf.dtype)
+            for j in range(LANES // rows):
+                a = columns[i * (LANES // rows) + j]
+                o_buf[:, a : a + HEAD_WIDTH] = turned[j * rows : (j + 1) * rows]
 
     held = []
 
@@ -256,7 +263,7 @@
             pltpu.VMEM((key_heads, reach + own_rows, HEAD_WIDTH), keys.dtype),
             pltpu.VMEM((key_heads, reach + own_rows, HEAD_WIDTH), values.dtype),
             pltpu.VMEM(lengths.shape, lengths.dtype),
-            pltpu.VMEM((rows, reach), jnp.float32),
+            pltpu.VMEM((reach, LANES), jnp.float32),
             pltpu.SemaphoreType.DMA((hops + 1, key_heads, 2)),
             pltpu.SemaphoreType.DMA((hops, key_heads, 2)),
             pltpu.SemaphoreType.DMA((2 + 2 * key_heads,)),

time: 13.1 us -> 12.8 us (0.977)
  Pallas kernels: 11.9 us -> 11.6 us
    pallas_call x1, Pallas kernels: 11.9 us -> 11.6 us  [local(): pl.pallas_call(functools.partial(kernel, sizes), out_shape=pltpu.VMEM(que...]
where the time goes in v5:
time: 12.8 us; the launch traced here: 12.6 us
  Pallas kernels  11.6 us (91%)
  local copies, waits for them, and re-layouts  0.97 us (8%)
    pallas_call x1, Pallas kernels, local(): pl.pallas_call(functools.partial(kernel, sizes), out_shape=pltpu.VMEM(que...  11.6 us
    unnamed x1, local copies, waits for them, and re-layouts  0.97 us

profile of v5, /device:TPU:29, one launch (start us, length us, event | category | flops | bytes accessed | tf_op | source)
XLA Modules:
  0.0 12.6 jit_solution(5871701819823774215)
XLA Ops:
  0.0 11.6 %ring_attention.1 = bf16[128,4096]{1,0:T(8,128)(2,1)S(1)} custom-call(bf16[128,4096]{1,0:T(8,128)(2,1)} %q_hbm.1, bf16[128,512]{1,0:T(8,128)(2,1)} %k_hbm.1, bf16[128,512]{1,0:T(8,128)(2,1)} %v_hbm.1, s32[2,128]{1,0:T(2,128)} %bitcast.1), custom_call_target="tpu_custom_call" | custom-call | tf_op jit(solution)/shard_map/ring_attention/pallas_call | solution.py:256
  11.6 1.0 %copy.6 = bf16[128,4096]{1,0:T(8,128)(2,1)} copy(bf16[128,4096]{1,0:T(8,128)(2,1)S(1)} %ring_attention.1) | data formatting | bytes 2097152

commit v6 on v5

--- a/solution.py
+++ b/solution.py
@@ -158,10 +158,20 @@
         for copy in found:
             copy.wait_send()
 
-    if paired:
-        for group in range(key_heads):
-            pl.when(has_second)(functools.partial(start_all, skipping(group)))
-            pl.when(has_next)(functools.partial(start_all, copies[0][group]))
+    straight = jnp.logical_and(jnp.logical_not(lead), has_next)
+
+    def start_far(group):
+        pl.when(has_second)(functools.partial(start_all, skipping(group)))
+        pl.when(straight)(functools.partial(start_all, copies[0][group]))
+
+    def pace(group):
+        def swap(done, following_ones):
+            for one, other in zip(done, following_ones):
+                one.wait_send()
+                other.start()
+
+        pl.when(has_second)(functools.partial(swap, skipping(group), skipping(group + 1)))
+        pl.when(straight)(functools.partial(swap, copies[0][group], copies[0][group + 1]))
 
     factor = math.log2(math.e) / math.sqrt(HEAD_WIDTH)
     own = lax.broadcasted_iota(jnp.int32, (own_rows, LANES), 0) <= lax.rem(
@@ -226,10 +236,33 @@
         if group < key_heads:
             held.append(weigh(group))
 
+    if paired:
+        start_far(0)
+        for group in range(key_heads):
+            pl.when(lead)(functools.partial(start_all, copies[0][group]))
+        paced = 0
+        for group in range(key_heads):
+            if group == 0 and key_heads > 1:
+                pace(0)
+                paced = 1
+            send(1, group)
+            if paced < key_heads - 1:
+                pace(paced)
+                paced += 1
+            attend(group)
+        attend(key_heads)
+        last = key_heads - 1
+        pl.when(has_second)(functools.partial(wait_sent, skipping(last)))
+        pl.when(straight)(functools.partial(wait_sent, copies[0][last]))
+        for group in range(key_heads):
+            pl.when(lead)(functools.partial(wait_sent, copies[0][group]))
+            pl.when(sends(1))(functools.partial(wait_sent, copies[1][group]))
+        return
+
     events = []
     for group in range(key_heads + 1):
         if group < key_heads:
-            for hop in range(1 if paired else 0, hops):
+            for hop in range(hops):
                 events.append((20 * group + 30 * hop, functools.partial(send, hop, group)))
         events.append((20 * group + 30 * hops + 2, functools.partial(attend, group)))
     for _, event in sorted(events, key=lambda pair: pair[0]):
@@ -237,8 +270,6 @@
     for group in range(key_heads):
         for hop in range(hops):
             pl.when(sends(hop))(functools.partial(wait_sent, copies[hop][group]))
-        if paired:
-            pl.when(has_second)(functools.partial(wait_sent, skipping(group)))
 
 
 def local(sizes, queries, keys, values, doc_lengths):

time: 12.8 us -> 13.5 us (1.055)
  the two profiles are of different devices: /device:TPU:29 before, /device:TPU:23 now
where the time goes in v6:
time: 13.5 us; the launch traced here: 13.3 us
  Pallas kernels  12.3 us (91%)
  local copies, waits for them, and re-layouts  0.97 us (7%)
    pallas_call x1, Pallas kernels, local(): pl.pallas_call(functools.partial(kernel, sizes), out_shape=pltpu.VMEM(que...  12.3 us
    unnamed x1, local copies, waits for them, and re-layouts  0.97 us

profile of v6, /device:TPU:23, one launch (start us, length us, event | category | flops | bytes accessed | tf_op | source)
XLA Modules:
  0.0 13.3 jit_solution(745960716924085612)
XLA Ops:
  0.0 12.3 %ring_attention.1 = bf16[128,4096]{1,0:T(8,128)(2,1)S(1)} custom-call(bf16[128,4096]{1,0:T(8,128)(2,1)} %q_hbm.1, bf16[128,512]{1,0:T(8,128)(2,1)} %k_hbm.1, bf16[128,512]{1,0:T(8,128)(2,1)} %v_hbm.1, s32[2,128]{1,0:T(2,128)} %bitcast.1), custom_call_target="tpu_custom_call" | custom-call | tf_op jit(solution)/shard_map/ring_attention/pallas_call | solution.py:287
  12.3 1.0 %copy.6 = bf16[128,4096]{1,0:T(8,128)(2,1)} copy(bf16[128,4096]{1,0:T(8,128)(2,1)S(1)} %ring_attention.1) | data formatting | bytes 2097152

commit v7 on v5

--- a/solution.py
+++ b/solution.py
@@ -43,8 +43,19 @@
     return starts
 
 
-def kernel(sizes, q_hbm, k_hbm, v_hbm, len_hbm, o_buf, q_buf, k_buf, v_buf, len_buf, bias,
-           send_sem, recv_sem, in_sem):
+def weigh_values(values, weights, inverses, out, first_column, rows):
+    summed = jnp.dot(jnp.transpose(values), weights, preferred_element_type=jnp.float32)
+    per_chunk = LANES // rows
+    for i, inverse in enumerate(inverses):
+        part = summed[:, i * LANES : (i + 1) * LANES] * inverse
+        turned = jnp.transpose(part).astype(out.dtype)
+        for j in range(per_chunk):
+            a = first_column + (i * per_chunk + j) * HEAD_WIDTH
+            out[:, a : a + HEAD_WIDTH] = turned[j * rows : (j + 1) * rows]
+
+
+def kernel(sizes, q_hbm, k_hbm, v_hbm, len_hbm, o_buf, last_weights, last_inverses, last_values,
+           q_buf, k_buf, v_buf, len_buf, bias, send_sem, recv_sem, in_sem):
     outer_count, inner_count, head_count = sizes
     rows, kv_width = k_hbm.shape
     key_heads = kv_width // HEAD_WIDTH
@@ -202,15 +213,13 @@
         return jnp.concatenate(weights, axis=1), inverses
 
     def gather(group, weights, inverses):
-        summed = jnp.dot(
-            jnp.transpose(v_buf[group]), weights, preferred_element_type=jnp.float32)
-        columns = columns_of(group)
-        for i in range(chunks):
-            part = summed[:, i * LANES : (i + 1) * LANES] * inverses[i]
-            turned = jnp.transpose(part).astype(o_buf.dtype)
-            for j in range(LANES // rows):
-                a = columns[i * (LANES // rows) + j]
-                o_buf[:, a : a + HEAD_WIDTH] = turned[j * rows : (j + 1) * rows]
+        if group < key_heads - 1:
+            weigh_values(v_buf[group], weights, inverses, o_buf, group * group_width, rows)
+            return
+        last_weights[...] = weights
+        last_values[...] = v_buf[group]
+        for i, inverse in enumerate(inverses):
+            last_inverses[i : i + 1, :] = inverse
 
     held = []
 
@@ -241,6 +250,18 @@
             pl.when(has_second)(functools.partial(wait_sent, skipping(group)))
 
 
+def finish(early, weights, inverses, values, o_hbm, late, sems):
+    rows, width = early.shape
+    early_copy = pltpu.make_async_copy(early, o_hbm.at[:, pl.ds(0, width)], sems.at[0])
+    early_copy.start()
+    parts = [inverses[i : i + 1, :] for i in range(inverses.shape[0])]
+    weigh_values(values[...], weights[...], parts, late, 0, rows)
+    late_copy = pltpu.make_async_copy(late, o_hbm.at[:, pl.ds(width, late.shape[1])], sems.at[1])
+    late_copy.start()
+    early_copy.wait()
+    late_copy.wait()
+
+
 def local(sizes, queries, keys, values, doc_lengths):
     rows, kv_width = keys.shape
     key_heads = kv_width // HEAD_WIDTH
@@ -253,11 +274,20 @@
         for value in (queries, keys, values, lengths)
     ]
     in_hbm = pl.BlockSpec(memory_space=pltpu.HBM)
-    return pl.pallas_call(
+    group_width = QUERY_PER_KEY * HEAD_WIDTH
+    early_width = (key_heads - 1) * group_width
+    chunks = QUERY_PER_KEY * rows // LANES
+    in_vmem = pl.BlockSpec(memory_space=pltpu.VMEM)
+    found = pl.pallas_call(
         functools.partial(kernel, sizes),
-        out_shape=pltpu.VMEM(queries.shape, queries.dtype),
+        out_shape=[
+            pltpu.VMEM((rows, early_width), queries.dtype),
+            pltpu.VMEM((reach + own_rows, chunks * LANES), jnp.bfloat16),
+            pltpu.VMEM((chunks, LANES), jnp.float32),
+            pltpu.VMEM((reach + own_rows, HEAD_WIDTH), values.dtype),
+        ],
         in_specs=[in_hbm, in_hbm, in_hbm, in_hbm],
-        out_specs=pl.BlockSpec(memory_space=pltpu.VMEM),
+        out_specs=[in_vmem] * 4,
         scratch_shapes=[
             pltpu.VMEM(queries.shape, queries.dtype),
             pltpu.VMEM((key_heads, reach + own_rows, HEAD_WIDTH), keys.dtype),
@@ -272,6 +302,18 @@
             collective_id=0, has_side_effects=True, vmem_limit_bytes=40 * 1024 * 1024),
         name="ring_attention",
     )(*operands)
+    return pl.pallas_call(
+        finish,
+        out_shape=jax.ShapeDtypeStruct(queries.shape, queries.dtype),
+        in_specs=[in_vmem] * 4,
+        out_specs=in_hbm,
+        scratch_shapes=[
+            pltpu.VMEM((rows, group_width), queries.dtype),
+            pltpu.SemaphoreType.DMA((2,)),
+        ],
+        compiler_params=pltpu.CompilerParams(vmem_limit_bytes=16 * 1024 * 1024),
+        name="write_result",
+    )(*[pltpu.with_memory_space_constraint(value, pltpu.VMEM) for value in found])
 
 
 def solution(mesh):

time: 12.8 us -> 12.6 us (0.984)
  local copies, waits for them, and re-layouts: 0.97 us -> 0 us
  Pallas kernels: 11.6 us -> 12.4 us
    unnamed x1 -> x0, local copies, waits for them, and re-layouts: 0.97 us -> none
    pallas_call x1 -> x2, Pallas kernels: 11.6 us -> 12.4 us  [the longest x1 11.3 us: local(): pl.pallas_call(functools.partial(kernel, sizes), out_shape=[pltpu.VMEM((r...]
where the time goes in v7:
time: 12.6 us; the launch traced here: 12.4 us
  Pallas kernels  12.4 us (98%)
    pallas_call x1, Pallas kernels, local(): pl.pallas_call(functools.partial(kernel, sizes), out_shape=[pltpu.VMEM((r...  11.3 us
    pallas_call x1, Pallas kernels, local(): pl.pallas_call(finish, out_shape=jax.ShapeDtypeStruct(queries.shape, quer...  1.13 us

profile of v7, /device:TPU:29, one launch (start us, length us, event | category | flops | bytes accessed | tf_op | source)
XLA Modules:
  0.0 12.4 jit_solution(7009701971145032345)
XLA Ops:
  0.0 11.3 %ring_attention.1 = (bf16[128,3072]{1,0:T(8,128)(2,1)S(1)}, bf16[384,1024]{1,0:T(8,128)(2,1)S(1)}, f32[8,128]{1,0:T(8,128)S(1)}, bf16[384,128]{1,0:T(8,128)(2,1)S(1)}) custom-call(bf16[128,4096]{1,0:T(8,128)(2,1)} %q_hbm.1, bf16[128,512]{1,0:T(8,128)(2,1)} %k_hbm.1, bf16[128,512]{1,0:T(8,128)(2,1)} %v_hbm.1, s32[2,128]{1,0:T(2,128)} %bitcast.1), custom_call_target="tpu_custom_call" | custom-call | tf_op jit(solution)/shard_map/ring_attention/pallas_call | solution.py:281
  11.3 1.1 %write_result.1 = bf16[128,4096]{1,0:T(8,128)(2,1)} custom-call(bf16[128,3072]{1,0:T(8,128)(2,1)S(1)} %get-tuple-element.9.early, bf16[384,1024]{1,0:T(8,128)(2,1)S(1)} %get-tuple-element.10.weights, f32[8,128]{1,0:T(8,128)S(1)} %get-tuple-element.11.inverses, bf16[384,128]{1,0:T(8,128)(2,1)S(1)} %get-tuple-element.12.values), custom_call_target="tpu_custom_call" | custom-call | tf_op jit(solution)/shard_map/write_result/pallas_call | solution.py:305

commit v8 on v7

--- a/solution.py
+++ b/solution.py
@@ -48,7 +48,7 @@
     per_chunk = LANES // rows
     for i, inverse in enumerate(inverses):
         part = summed[:, i * LANES : (i + 1) * LANES] * inverse
-        turned = jnp.transpose(part).astype(out.dtype)
+        turned = jnp.transpose(part.astype(out.dtype))
         for j in range(per_chunk):
             a = first_column + (i * per_chunk + j) * HEAD_WIDTH
             out[:, a : a + HEAD_WIDTH] = turned[j * rows : (j + 1) * rows]
@@ -169,10 +169,26 @@
         for copy in found:
             copy.wait_send()
 
+    straight = jnp.logical_and(jnp.logical_not(lead), has_next)
+    ahead = min(2, key_heads)
+
+    def swap(done, later):
+        for one, other in zip(done, later):
+            one.wait_send()
+            other.start()
+
+    def pace(group):
+        later = group + ahead
+        if later < key_heads:
+            pl.when(has_second)(functools.partial(swap, skipping(group), skipping(later)))
+            pl.when(straight)(functools.partial(swap, copies[0][group], copies[0][later]))
+
     if paired:
+        for group in range(ahead):
+            pl.when(has_second)(functools.partial(start_all, skipping(group)))
+            pl.when(straight)(functools.partial(start_all, copies[0][group]))
         for group in range(key_heads):
-            pl.when(has_second)(functools.partial(start_all, skipping(group)))
-            pl.when(has_next)(functools.partial(start_all, copies[0][group]))
+            pl.when(lead)(functools.partial(start_all, copies[0][group]))
 
     factor = math.log2(math.e) / math.sqrt(HEAD_WIDTH)
     own = lax.broadcasted_iota(jnp.int32, (own_rows, LANES), 0) <= lax.rem(
@@ -185,6 +201,8 @@
         return jnp.logical_and(there, lead) if paired and hop > 0 else there
 
     def send(hop, group):
+        if paired:
+            pace(group)
         for at, copy in enumerate(copies[hop][group]):
             if hop > 0:
                 pl.when(piece >= hop)(copies[hop - 1][group][at].wait_recv)
@@ -245,9 +263,13 @@
         event()
     for group in range(key_heads):
         for hop in range(hops):
-            pl.when(sends(hop))(functools.partial(wait_sent, copies[hop][group]))
-        if paired:
-            pl.when(has_second)(functools.partial(wait_sent, skipping(group)))
+            if paired and hop == 0:
+                pl.when(lead)(functools.partial(wait_sent, copies[0][group]))
+                if group + ahead >= key_heads:
+                    pl.when(has_second)(functools.partial(wait_sent, skipping(group)))
+                    pl.when(straight)(functools.partial(wait_sent, copies[0][group]))
+            else:
+                pl.when(sends(hop))(functools.partial(wait_sent, copies[hop][group]))
 
 
 def finish(early, weights, inverses, values, o_hbm, late, sems):

time: 12.6 us -> 12.5 us (level)
  no operation moved by 1% of the time
where the time goes in v8:
time: 12.5 us; the launch traced here: 12.4 us
  Pallas kernels  12.4 us (99%)
    pallas_call x1, Pallas kernels, local(): pl.pallas_call(functools.partial(kernel, sizes), out_shape=[pltpu.VMEM((r...  11.3 us
    pallas_call x1, Pallas kernels, local(): pl.pallas_call(finish, out_shape=jax.ShapeDtypeStruct(queries.shape, quer...  1.12 us

profile of v8, /device:TPU:29, one launch (start us, length us, event | category | flops | bytes accessed | tf_op | source)
XLA Modules:
  0.0 12.4 jit_solution(4699172770244686132)
XLA Ops:
  0.0 11.3 %ring_attention.1 = (bf16[128,3072]{1,0:T(8,128)(2,1)S(1)}, bf16[384,1024]{1,0:T(8,128)(2,1)S(1)}, f32[8,128]{1,0:T(8,128)S(1)}, bf16[384,128]{1,0:T(8,128)(2,1)S(1)}) custom-call(bf16[128,4096]{1,0:T(8,128)(2,1)} %q_hbm.1, bf16[128,512]{1,0:T(8,128)(2,1)} %k_hbm.1, bf16[128,512]{1,0:T(8,128)(2,1)} %v_hbm.1, s32[2,128]{1,0:T(2,128)} %bitcast.1), custom_call_target="tpu_custom_call" | custom-call | tf_op jit(solution)/shard_map/ring_attention/pallas_call | solution.py:303
  11.3 1.1 %write_result.1 = bf16[128,4096]{1,0:T(8,128)(2,1)} custom-call(bf16[128,3072]{1,0:T(8,128)(2,1)S(1)} %get-tuple-element.9.early, bf16[384,1024]{1,0:T(8,128)(2,1)S(1)} %get-tuple-element.10.weights, f32[8,128]{1,0:T(8,128)S(1)} %get-tuple-element.11.inverses, bf16[384,128]{1,0:T(8,128)(2,1)S(1)} %get-tuple-element.12.values), custom_call_target="tpu_custom_call" | custom-call | tf_op jit(solution)/shard_map/write_result/pallas_call | solution.py:327

commit v9 on v8

--- a/solution.py
+++ b/solution.py
@@ -193,6 +193,7 @@
     factor = math.log2(math.e) / math.sqrt(HEAD_WIDTH)
     own = lax.broadcasted_iota(jnp.int32, (own_rows, LANES), 0) <= lax.rem(
         lax.broadcasted_iota(jnp.int32, (own_rows, LANES), 1), rows)
+    own_mask = jnp.where(own, 1.0, 0.0).astype(jnp.bfloat16)
     chunks = QUERY_PER_KEY * rows // LANES
     group_width = QUERY_PER_KEY * HEAD_WIDTH
 
@@ -225,9 +226,10 @@
             first = jnp.exp2(first * factor - top)
             rest = jnp.exp2(rest * factor - top)
             inverses.append(1.0 / jnp.sum(first + rest, axis=0, keepdims=True))
+            rounded = first.astype(jnp.bfloat16)
+            near = rounded * own_mask
             weights.append(jnp.concatenate(
-                [jnp.where(own, 0.0, first).astype(jnp.bfloat16), rest.astype(jnp.bfloat16),
-                 jnp.where(own, first, 0.0).astype(jnp.bfloat16)], axis=0))
+                [rounded - near, rest.astype(jnp.bfloat16), near], axis=0))
         return jnp.concatenate(weights, axis=1), inverses
 
     def gather(group, weights, inverses):
@@ -277,11 +279,21 @@
     early_copy = pltpu.make_async_copy(early, o_hbm.at[:, pl.ds(0, width)], sems.at[0])
     early_copy.start()
     parts = [inverses[i : i + 1, :] for i in range(inverses.shape[0])]
-    weigh_values(values[...], weights[...], parts, late, 0, rows)
-    late_copy = pltpu.make_async_copy(late, o_hbm.at[:, pl.ds(width, late.shape[1])], sems.at[1])
-    late_copy.start()
+    half = late.shape[1] // 2
+    per_half = len(parts) // 2
+    late_copies = []
+    for i in range(2):
+        lanes = slice(i * per_half * LANES, (i + 1) * per_half * LANES)
+        weigh_values(
+            values[...], weights[:, lanes], parts[i * per_half : (i + 1) * per_half],
+            late, i * half, rows)
+        late_copies.append(pltpu.make_async_copy(
+            late.at[:, pl.ds(i * half, half)], o_hbm.at[:, pl.ds(width + i * half, half)],
+            sems.at[1 + i]))
+        late_copies[i].start()
     early_copy.wait()
-    late_copy.wait()
+    for copy in late_copies:
+        copy.wait()
 
 
 def local(sizes, queries, keys, values, doc_lengths):
@@ -331,7 +343,7 @@
         out_specs=in_hbm,
         scratch_shapes=[
             pltpu.VMEM((rows, group_width), queries.dtype),
-            pltpu.SemaphoreType.DMA((2,)),
+            pltpu.SemaphoreType.DMA((3,)),
         ],
         compiler_params=pltpu.CompilerParams(vmem_limit_bytes=16 * 1024 * 1024),
         name="write_result",

time: 12.5 us -> 12.5 us (level)
  no operation moved by 1% of the time
where the time goes in v9:
time: 12.5 us; the launch traced here: 12.4 us
  Pallas kernels  12.4 us (99%)
    pallas_call x1, Pallas kernels, local(): pl.pallas_call(functools.partial(kernel, sizes), out_shape=[pltpu.VMEM((r...  11.3 us
    pallas_call x1, Pallas kernels, local(): pl.pallas_call(finish, out_shape=jax.ShapeDtypeStruct(queries.shape, quer...  1.1 us

profile of v9, /device:TPU:29, one launch (start us, length us, event | category | flops | bytes accessed | tf_op | source)
XLA Modules:
  0.0 12.4 jit_solution(1558310117751356961)
XLA Ops:
  0.0 11.3 %ring_attention.1 = (bf16[128,3072]{1,0:T(8,128)(2,1)S(1)}, bf16[384,1024]{1,0:T(8,128)(2,1)S(1)}, f32[8,128]{1,0:T(8,128)S(1)}, bf16[384,128]{1,0:T(8,128)(2,1)S(1)}) custom-call(bf16[128,4096]{1,0:T(8,128)(2,1)} %q_hbm.1, bf16[128,512]{1,0:T(8,128)(2,1)} %k_hbm.1, bf16[128,512]{1,0:T(8,128)(2,1)} %v_hbm.1, s32[2,128]{1,0:T(2,128)} %bitcast.1), custom_call_target="tpu_custom_call" | custom-call | tf_op jit(solution)/shard_map/ring_attention/pallas_call | solution.py:315
  11.3 1.1 %write_result.1 = bf16[128,4096]{1,0:T(8,128)(2,1)} custom-call(bf16[128,3072]{1,0:T(8,128)(2,1)S(1)} %get-tuple-element.9.early, bf16[384,1024]{1,0:T(8,128)(2,1)S(1)} %get-tuple-element.10.weights, f32[8,128]{1,0:T(8,128)S(1)} %get-tuple-element.11.inverses, bf16[384,128]{1,0:T(8,128)(2,1)S(1)} %get-tuple-element.12.values), custom_call_target="tpu_custom_call" | custom-call | tf_op jit(solution)/shard_map/write_result/pallas_call | solution.py:339
